TPU v7x, 128 devices: a whole 4x4x4 slice. The times are simulated.
128 devices in a mesh: gx: 8 (over x, core), gy: 16 (over z, y).
Axes of the slice: x: 4, y: 4, z: 4, core: 2. Of those that a mesh axis runs over, the one named last changes fastest.
Arguments:
- multipoles: bfloat16 [32768, 121], P(('gx', 'gy')), may hold values from -6 to 6
- m2l_ops: bfloat16 [316, 121, 121], replicated, may hold values from -0.0625 to 0.0625
- want_boxes: int32 [128, 16, 128], P(('gx', 'gy')), may hold values from 0 to 255
- m2l_source: int32 [32768, 189], P(('gx', 'gy')), may hold values from 0 to 2303, as said below
- m2l_offset: int32 [32768, 189], P(('gx', 'gy')), may hold values from 0 to 315, as said below
- m2l_count: int32 [32768], P(('gx', 'gy')), may hold values from 1 to 189, as said below
- positions: float32 [32768, 3, 128], P(('gx', 'gy')), may hold values from 0 to 1
- charges: float32 [32768, 128], P(('gx', 'gy')), may hold values from -6 to 6
- part_count: int32 [32768], P(('gx', 'gy')), may hold values from 1 to 128
- pair_target: int32 [128, 1024], P(('gx', 'gy')), may hold values from 0 to 255
- pair_source: int32 [128, 1024], P(('gx', 'gy')), may hold values from 0 to 511, as said below
- pair_offset: int32 [128, 1024], P(('gx', 'gy')), may hold values from 0 to 26, as said below
- pair_count: int32 [128], P(('gx', 'gy')), may hold values from 1 to 1024, as said below
Outputs:
- local_exp: float32 [32768, 121], P(('gx', 'gy'))
- near_field: float32 [32768, 128], P(('gx', 'gy'))
Inputs may be any that keep to these rules, and one draw needn't show every extreme that they name: `m2l_offset`: the 189 offset numbers of one box are distinct. Slots k >= m2l_count[t] of a box's interaction list are unused. `m2l_source`: an entry of box t on device d that names reach n has 0 <= d + rel(n) < 0 + number of devices, so only devices inside the mesh are named. Slots k >= pair_count[d] of device d are unused. `pair_source`: on the last device every entry is below 256. `pair_offset`: never 13.
All inputs are finite; a program needn't handle non-finite values.
Results may differ from a plain program's by a relative error of at most 0.0003.
Values may be sent and summed in bfloat16 or wider, within the bound.
No kernel may reach another device: no remote copies, remote signals or barrier semaphores. Data moves between devices by JAX's collectives and lax.ppermute only.
A program may use at most 128 MiB of HBM per device.

v0:
```python
import functools

import jax
import jax.numpy as jnp
from jax import lax
from jax.experimental import pallas as pl
from jax.experimental.pallas import tpu as pltpu
from jax.sharding import PartitionSpec as P

BOX, PB, EPS = 256, 128, 0.0025
OFFS, OP, KMAX, KP, COEF, NEAR, CAP = 316, 320, 189, 208, 121, 16, 128
ZROW = BOX + NEAR * CAP
NTAB = ZROW + 8
DROW = OFFS * BOX
LST = 3200
f32, bf16 = jnp.float32, jnp.bfloat16
AXES = ("gx", "gy")

def split3(v):
    a=v.astype(bf16).astype(f32); r=v-a
    b=r.astype(bf16).astype(f32); c=r-b
    return a,b,c

def near_body(U,PU,tgt_ref,src_ref,off_ref,cnt_ref,own_ref,nxt_ref,tcol_ref,srow_ref,out_ref,fwd_ref,xb,fa,qa,cc,dd,vv):
    sub=lax.broadcasted_iota(jnp.int32,(8,128),0)
    m3=(sub<3).astype(f32)
    one=jnp.ones((8,128),f32); zero=jnp.zeros((8,128),f32)
    for o in range(27):
        v=(o//9-1,(o//3)%3-1,o%3-1)
        vv[o]=jnp.where(sub==0,float(v[0]),jnp.where(sub==1,float(v[1]),jnp.where(sub==2,float(v[2]),0.0)))
    def rows(g,_):
        for half,ref in ((0,own_ref),(1,nxt_ref)):
            for c in range(4):
                p=ref[c,pl.ds(pl.multiple_of(g*8,8),8),:]
                if c<3: p=p-0.5
                xb[pl.ds(half*BOX*8+g*64+c,8,stride=8),:]=p
            for c in range(4,8):
                xb[pl.ds(half*BOX*8+g*64+c,8,stride=8),:]=zero
        return 0
    lax.fori_loop(0,BOX//8,rows,0)
    def feat_b(y):
        y1,y2,y3=split3(y)
        q1,q2,q3=split3(y*y)
        return jnp.concatenate([y1,y1,y1,y2,y2,y3,q1,q2,q3,one]+[zero]*6,0).astype(bf16)
    diag=lax.broadcasted_iota(jnp.int32,(PB,PB),0)==lax.broadcasted_iota(jnp.int32,(PB,PB),1)
    def sq(b):
        return xb[pl.ds(pl.multiple_of(b*8,8),8),:]
    def prep(g,_):
        for u in range(PU):
            b=g*PU+u
            x=sq(b)
            x1,x2,x3=split3(x*-2.0)
            xm=x*m3
            s=jnp.sum(xm*xm,axis=0,keepdims=True)+EPS
            s=jnp.broadcast_to(s,(8,128))
            s1,s2,s3=split3(s)
            sr=jnp.where(sub==0,s1,jnp.where(sub==1,s2,jnp.where(sub==2,s3,0.0)))
            x1,x2,x3=x1*m3,x2*m3,x3*m3
            f=jnp.concatenate([x1,x2,x3,x1,x2,x1,m3,m3,m3,sr,x]+[zero]*5,0)
            t=f.T
            ft=jnp.where(lax.broadcasted_iota(jnp.int32,(PB,128),1)<80,t,0.0).astype(bf16)
            fa[b]=ft
            q=jnp.broadcast_to(t[:,83:84],(PB,PB))
            qa[b]=q
            k=lax.rsqrt(jnp.dot(ft,feat_b(x),preferred_element_type=f32))
            k=jnp.where(diag,0.0,k)
            out_ref[pl.ds(b,1),:]=jnp.sum(k*q,axis=0,keepdims=True)
        return 0
    lax.fori_loop(0,BOX//PU,prep,0)
    n=cnt_ref[0]
    def zinit(i,_):
        dd[pl.ds(pl.multiple_of(i*8,8),8),:]=zero
        cc[pl.ds(pl.multiple_of(i*8,8),8),:]=zero
        return 0
    lax.fori_loop(0,128,zinit,0)
    lane=lax.broadcasted_iota(jnp.int32,(PB,128),1)
    if True:
        def pairs(g,_):
            cs=[]
            for u in range(U):
                p=g*U+u
                a=tgt_ref[p]; b=src_ref[p]; o=off_ref[p]
                y=sq(b)+vv[o]
                k=lax.rsqrt(jnp.dot(fa[a],feat_b(y),preferred_element_type=f32))
                qb=xb[pl.ds(b*8+3,1),:]
                dd[pl.ds(p,1),:]=jnp.sum(k*qa[a],axis=0,keepdims=True)
                cs.append(jnp.sum(k*qb,axis=1,keepdims=True))
            blk=lax.shift_right_logical(g*U,7)
            l0=(g*U)&127
            r=pl.ds(pl.multiple_of(blk*128,128),128)
            c=cc[r,:]
            for u in range(U):
                c=jnp.where(lane==l0+u,cs[u],c)
            cc[r,:]=c
            return 0
        lax.fori_loop(0,lax.div(n+U-1,U),pairs,0)
    fwd_ref[...]=jnp.zeros_like(fwd_ref)
    def scat(k,_):
        r=pl.ds(pl.multiple_of(k*128,128),128)
        prow=k*128+lax.broadcasted_iota(jnp.int32,(1,128),1)
        tid=jnp.where(prow<n,tcol_ref[pl.ds(k,1),:],-1)
        sid=jnp.where(prow<n,srow_ref[pl.ds(k,1),:],-1)
        oh_t=(lax.broadcasted_iota(jnp.int32,(BOX,128),0)==tid).astype(f32).astype(bf16)
        oh_s=(lax.broadcasted_iota(jnp.int32,(2*BOX,128),0)==sid).astype(f32).astype(bf16)
        c1,c2,c3=split3(cc[r,:])
        d1,d2,d3=split3(dd[r,:])
        nt=(((1,),(1,)),((),()))
        ct=sum(lax.dot_general(oh_t,c.astype(bf16),nt,preferred_element_type=f32) for c in (c1,c2,c3))
        ds=sum(jnp.dot(oh_s,d.astype(bf16),preferred_element_type=f32) for d in (d1,d2,d3))
        out_ref[...]+=ct+ds[:BOX]
        fwd_ref[...]+=ds[BOX:]
        return 0
    lax.fori_loop(0,lax.div(n+127,128),scat,0)

def near(tgt,src,off,cnt,own4,nxt4,U=32,PU=16):
    sm=pl.BlockSpec(memory_space=pltpu.SMEM); vm=pl.BlockSpec(memory_space=pltpu.VMEM)
    return pl.pallas_call(functools.partial(near_body,U,PU),
        out_shape=(jax.ShapeDtypeStruct((BOX,PB),f32),jax.ShapeDtypeStruct((BOX,PB),f32)),
        in_specs=[sm]*4+[vm]*4,
        out_specs=(vm,vm),
        scratch_shapes=[pltpu.VMEM((2*BOX*8,128),f32),pltpu.VMEM((BOX,PB,128),bf16),pltpu.VMEM((BOX,PB,128),f32),
            pltpu.VMEM((1024,128),f32),pltpu.VMEM((1024,128),f32),pltpu.VMEM((27,8,128),f32)],
        compiler_params=pltpu.CompilerParams(vmem_limit_bytes=56<<20),
        name="near")(tgt,src,off,cnt,own4,nxt4,tgt.reshape(8,128),src.reshape(8,128))

def swap8(rows,masks):
    rows=list(rows)
    for s,m in zip((4,2,1),masks):
        for i in range(8):
            if i&s: continue
            a,b=rows[i],rows[i+s]
            rows[i]=jnp.where(m,a,pltpu.roll(b,s,0))
            rows[i+s]=jnp.where(m,pltpu.roll(a,8-s,0),b)
    return rows

def relayout_body(in_ref,out_ref,buf):
    OB=in_ref.shape[1]
    @pl.when(pl.program_id(0)==0)
    def _():
        buf[...]=jnp.zeros_like(buf)
    for c in range(COEF):
        buf[c*OB:(c+1)*OB,:COEF]=in_ref[c].astype(f32)
    sub=lax.broadcasted_iota(jnp.int32,(8,128),0)
    masks=[(sub&s)==0 for s in (4,2,1)]
    for o in range(0,OB,8):
        for c in range(0,128,16):
            lo=swap8([buf[(c+i)*OB+o:(c+i)*OB+o+8,:] for i in range(8)],masks)
            hi=swap8([buf[(c+8+i)*OB+o:(c+8+i)*OB+o+8,:] for i in range(8)],masks)
            for i in range(8):
                out_ref[o+i,c:c+16,:]=jnp.concatenate([lo[i],hi[i]],0).astype(bf16)

def relayout(ops_t,OB=32):
    return pl.pallas_call(relayout_body,
        out_shape=jax.ShapeDtypeStruct((OP,128,128),bf16),
        grid=(OP//OB,),
        in_specs=[pl.BlockSpec((COEF,OB,COEF),lambda i:(0,i,0))],
        out_specs=pl.BlockSpec((OB,128,128),lambda i:(i,0,0)),
        scratch_shapes=[pltpu.VMEM((128*OB,128),f32)],
        compiler_params=pltpu.CompilerParams(vmem_limit_bytes=40<<20),
        name="relayout")(ops_t)

def m2l_body(U,B,OG,num_ref,want_ref,blk_ref,src_hbm,dst_hbm,lst_hbm,own_hbm,ag_hbm,ops_hbm,out_ref,
             src_ref,dst_ref,lst_ref,own_ref,ag_ref,ops,tab,tmp,dense,sem):
    T=BOX
    cps=[pltpu.make_async_copy(a,b,sem.at[i]) for i,(a,b) in enumerate(
        ((own_hbm,own_ref),(ag_hbm,ag_ref),(src_hbm,src_ref),(dst_hbm,dst_ref),(lst_hbm,lst_ref),(ops_hbm,ops)))]
    for c in cps: c.start()
    def zero(i,_):
        dense[pl.ds(pl.multiple_of(i*512,512),512),:]=jnp.zeros((512,128),f32)
        return 0
    lax.fori_loop(0,OFFS*T//512,zero,0)
    cps[0].wait()
    cps[1].wait()
    tab[0:BOX,:]=own_ref[...].astype(f32)
    tab[ZROW:ZROW+8,:]=jnp.zeros((8,128),f32)
    def reach(n,_):
        r0=pl.multiple_of(blk_ref[n]*BOX,BOX)
        tmp[...]=ag_ref[pl.ds(r0,BOX),:].astype(f32)
        d0=pl.multiple_of(BOX+n*CAP,8)
        for u in range(CAP):
            w=want_ref.at[pl.ds(u,(NEAR-1)*CAP+1)][n*CAP]
            tab[pl.ds(d0+u,1),:]=tmp[pl.ds(w,1),:]
        return 0
    lax.fori_loop(0,NEAR,reach,0)
    for c in cps[2:5]: c.wait()
    def chunk(i,_):
        for v in range(B):
            b=lst_ref.at[pl.ds(v,3072)][i*B]
            for u in range(U):
                w=pl.ds(u*BOX,(KP-U)*BOX+BOX)
                dense[pl.ds(dst_ref.at[w][b],1),:]=tab[pl.ds(src_ref.at[w][b],1),:]
        return 0
    lax.fori_loop(0,num_ref[0],chunk,0)
    cps[5].wait()
    out_ref[...]=jnp.zeros_like(out_ref)
    def part(o,n):
        ls=[dense[pl.ds(pl.multiple_of((o+j)*T,T),T),:].astype(bf16) for j in range(n)]
        r=ops[pl.ds(pl.multiple_of(o*128,128),n*128),:]
        out_ref[...]+=jnp.dot(jnp.concatenate(ls,1),r,preferred_element_type=f32)[:,:COEF]
    NS=OFFS//OG
    def mm(k,_):
        part(k*OG,OG)
        return 0
    lax.fori_loop(0,NS,mm,0)
    if OFFS%OG: part(NS*OG,OFFS%OG)

def m2l(src,dst,lst,num,want,blk,own,ag,ops,U=16,B=8,OG=20):
    sm=pl.BlockSpec(memory_space=pltpu.SMEM); vm=pl.BlockSpec(memory_space=pltpu.VMEM); hb=pl.BlockSpec(memory_space=pl.ANY)
    return pl.pallas_call(functools.partial(m2l_body,U,B,OG),
        out_shape=jax.ShapeDtypeStruct((BOX,COEF),f32),
        in_specs=[sm]*3+[hb]*6, out_specs=vm,
        scratch_shapes=[pltpu.SMEM((KP*BOX,),jnp.int32),pltpu.SMEM((KP*BOX,),jnp.int32),pltpu.SMEM((LST,),jnp.int32),
            pltpu.VMEM((BOX,128),bf16),pltpu.VMEM(ag.shape,bf16),pltpu.VMEM((OP*128,128),bf16),
            pltpu.VMEM((NTAB,128),f32),pltpu.VMEM((BOX,128),f32),pltpu.VMEM((DROW+8,128),f32),pltpu.SemaphoreType.DMA((6,))],
        compiler_params=pltpu.CompilerParams(vmem_limit_bytes=58<<20),
        name="m2l")(num,want,blk,src,dst,lst,own,ag,ops)

def slots(srcT,offT,cnt,U=16,B=8):
    k=lax.broadcasted_iota(jnp.int32,(KMAX,BOX),0)
    t=lax.broadcasted_iota(jnp.int32,(KMAX,BOX),1)
    s=jnp.where(k<cnt[None,:],srcT,ZROW)
    d=offT*BOX+t
    s=jnp.pad(s,((0,KP-KMAX),(0,0)),constant_values=ZROW).reshape(-1)
    d=jnp.pad(d,((0,KP-KMAX),(0,0)),constant_values=DROW).reshape(-1)
    n=lax.div(cnt+U-1,U)
    a=jnp.arange(BOX,dtype=jnp.int32)
    incl=jnp.sum(jnp.where(a[None,:]<=a[:,None],n[None,:],0),1)
    i=jnp.arange(LST,dtype=jnp.int32)
    m=incl[None,:]<=i[:,None]
    bx=jnp.sum(m.astype(jnp.int32),1)
    ex=jnp.sum(jnp.where(m,n[None,:],0),1)
    lst=jnp.where(bx<BOX,bx+(i-ex)*(U*BOX),192*BOX)
    num=lax.div(jnp.sum(n)+B-1,B)
    return s,d,lst,num[None]

def ring(x,by,n):
    return lax.ppermute(x,AXES,[(i,i+by) for i in range(n) if 0<=i+by<n])

def shards(gx,gy,multipoles,m2l_ops,want_boxes,m2l_source,m2l_offset,m2l_count,positions,charges,part_count,
           pair_target,pair_source,pair_offset,pair_count):
    n=gx*gy
    x,y=lax.axis_index("gx"),lax.axis_index("gy")
    live=lax.broadcasted_iota(jnp.int32,(BOX,PB),1)<part_count[:,None]
    own4=jnp.concatenate([positions.transpose(1,0,2),jnp.where(live,charges,0.0)[None]],0)
    nxt4=ring(own4,-1,n)
    own=jnp.pad(multipoles,((0,0),(0,128-COEF)))
    half=gy//2
    swap=[]
    for g in range(gx):
        for j in range(gy):
            to=g+1 if j>=half else g-1
            if 0<=to<gx: swap.append((g*gy+j,to*gy+j))
    other=lax.ppermute(own,AXES,swap)
    ag=lax.all_gather(jnp.stack([own,other]),"gy").reshape(-1,128)
    me=x*gy+y
    reach=jnp.arange(NEAR,dtype=jnp.int32)
    peer=jnp.clip(me+reach-NEAR//2+(reach>=NEAR//2).astype(jnp.int32),0,n-1)
    px,py=lax.div(peer,gy),lax.rem(peer,gy)
    blk=py*2+(px!=x).astype(jnp.int32)
    s,d,lst,num=slots(m2l_source.T,m2l_offset.T,m2l_count)
    ops=relayout(m2l_ops.transpose(1,0,2)).reshape(-1,128)
    nxt4,ops,s,d,lst,num,blk=lax.optimization_barrier((nxt4,ops,s,d,lst,num,blk))
    field,fwd=near(pair_target[0],pair_source[0],pair_offset[0],pair_count,own4,nxt4)
    back=ring(fwd,1,n)
    local_exp=m2l(s,d,lst,num,want_boxes.reshape(-1),blk,own,ag,ops)
    return local_exp,jnp.where(live,field+back,0.0)

def solution(mesh):
    both=AXES
    placed=(P(both,None),P(),P(both,None,None),P(both,None),P(both,None),P(both),P(both,None,None),P(both,None),P(both),
            P(both,None),P(both,None),P(both,None),P(both))
    return jax.shard_map(functools.partial(shards,mesh.shape["gx"],mesh.shape["gy"]),mesh=mesh,in_specs=placed,
        out_specs=(P(both,None),P(both,None)),check_vma=False)
```

profile of v0, /device:TPU:6, one launch (start us, length us, event | category | flops | bytes accessed | tf_op | source)
XLA Modules:
  0.0 151.4 jit_solution(2456608220839703491)
XLA Ops:
  7.2 0.0 all-gather.3.cloned.1.call-start
  7.2 0.9 pad_bitcast_fusion.2
  8.1 2.2 %collective-permute-start.1 = (bf16[256,128]{1,0:T(8,128)(2,1)S(1)}, bf16[256,128]{1,0:T(8,128)(2,1)S(1)}, u32[]{:S(2)}, u32[]{:S(2)}) collective-permute-start(bf16[256,128]{1,0:T(8,128)(2,1)S(1)} %get-tuple-element.25.own_hbm), channel_id=1, source_target_pairs={{8,24},{9,25},{10,26},{11,27},{12,28},{13,29},{14,30},{15,31},{16,... | collective-permute-start | bytes 196616 | tf_op jit(solution)/shard_map/ppermute | solution.py:253
  10.3 1.9 %collective-permute-done.1 = bf16[256,128]{1,0:T(8,128)(2,1)S(1)} collective-permute-done((bf16[256,128]{1,0:T(8,128)(2,1)S(1)}, bf16[256,128]{1,0:T(8,128)(2,1)S(1)}, u32[]{:S(2)}, u32[]{:S(2)}) %collective-permute-start.1) | collective-permute-done | bytes 65568 | tf_op jit(solution)/shard_map/ppermute | solution.py:253
  12.2 0.7 pad_maximum_fusion.1
  12.8 0.0 all-gather.3.cloned.1.call-update
  12.8 1.0 select_bitcast_fusion
  13.9 1.0 pad_maximum_fusion.own_ref
  14.9 8.7 %collective-permute-start = (f32[4,256,128]{2,1,0:T(8,128)S(1)}, f32[4,256,128]{2,1,0:T(8,128)S(1)}, u32[]{:S(2)}, u32[]{:S(2)}) collective-permute-start(f32[4,256,128]{2,1,0:T(8,128)S(1)} %pad_maximum_fusion.own_ref), channel_id=1, source_target_pairs={{1,0},{2,1},{3,2},{4,3},{5,4},{6,5},{7,6},{8,7},{9,8},{10,9},{11,1... | collective-permute-start | bytes 1572872 | tf_op jit(solution)/shard_map/ppermute | solution.py:237
  23.7 1.3 fusion.4
  25.7 3.9 %copy-done = bf16[316,121,121]{2,0,1:T(8,128)(2,1)S(1)} copy-done((bf16[316,121,121]{2,0,1:T(8,128)(2,1)S(1)}, bf16[316,121,121]{2,0,1:T(8,128)(2,1)}, u32[]{:S(2)}) %copy-start) | copy-done | bytes 9253136
  29.6 8.9 %relayout.1 = bf16[320,128,128]{2,1,0:T(8,128)(2,1)} custom-call(bf16[121,316,121]{2,1,0:T(8,128)(2,1)S(1)} %bitcast.26), custom_call_target="tpu_custom_call" | custom-call | tf_op jit(solution)/shard_map/relayout/pallas_call | solution.py:153
  38.6 0.8 copy.15
  39.5 0.8 copy.16
  40.9 0.1 select_reduce_fusion.1
  41.0 0.5 fusion.3.blk_ref
  41.6 1.1 select_reduce_fusion
  42.6 0.6 add_select_fusion.1.lst_hbm
  43.3 0.8 copy-done.2
  44.1 39.4 %near.1 = (f32[256,128]{1,0:T(8,128)}, f32[256,128]{1,0:T(8,128)}) custom-call(s32[1024]{0:T(1024)} %bitcast.33, s32[1024]{0:T(1024)} %bitcast.35, s32[1024]{0:T(1024)} %bitcast.38, s32[1]{0:T(128)S(6)} %copy.17.cnt_ref, f32[4,256,128]{2,1,0:T(8,128)} %copy-done.1, f32[4,256,128]{2,1,0:T(8,128)} %copy-done.2, s32[8,128]{1,0:T(8,128)} %bitcast.34, ...), custom_call_target="tpu_custom_call" | custom-call | tf_op jit(solution)/shard_map/near/pallas_call | solution.py:117
  83.5 1.9 %collective-permute-start.2 = (f32[256,128]{1,0:T(8,128)}, f32[256,128]{1,0:T(8,128)S(1)}, u32[]{:S(2)}, u32[]{:S(2)}) collective-permute-start(f32[256,128]{1,0:T(8,128)} %get-tuple-element.19), channel_id=1, source_target_pairs={{0,1},{1,2},{2,3},{3,4},{4,5},{5,6},{6,7},{7,8},{8,9},{9,10},{10,1... | collective-permute-start | bytes 393224 | tf_op jit(solution)/shard_map/ppermute | solution.py:237
  85.4 8.8 %collective-permute-done.2 = f32[256,128]{1,0:T(8,128)S(1)} collective-permute-done((f32[256,128]{1,0:T(8,128)}, f32[256,128]{1,0:T(8,128)S(1)}, u32[]{:S(2)}, u32[]{:S(2)}) %collective-permute-start.2) | collective-permute-done | bytes 131104 | tf_op jit(solution)/shard_map/ppermute | solution.py:237
  94.2 1.7 %add_select_fusion = f32[256,128]{1,0:T(8,128)} fusion(f32[256,128]{1,0:T(8,128)} %get-tuple-element.18, f32[256,128]{1,0:T(8,128)S(1)} %collective-permute-done.2, s32[256]{0:T(256)S(1)} %copy-done.6), kind=kLoop, calls=%fused_computation.12 | loop fusion | flops 98304 | bytes 394240 | tf_op jit(solution)/shard_map/jit(_where)/select_n | solution.py:266
  95.8 48.7 %m2l.1 = f32[256,121]{1,0:T(8,128)} custom-call(s32[1]{0:T(128)} %bitcast.6.num_ref, s32[2048]{0:T(1024)} %bitcast.37, s32[16]{0:T(128)} %fusion.3.blk_ref, s32[53248]{0:T(1024)} %bitcast.29, s32[53248]{0:T(1024)} %bitcast.30, s32[3200]{0:T(1024)} %add_select_fusion.1.lst_hbm, bf16[256,128]{1,0:T(8,128)(2,1)} %copy-done.3, bf16[8192,128]{1,0:T(8,128)(2,1)} %bitcast.28, ...), custom_call_target="tpu_custom_call" | custom-call | tf_op jit(solution)/shard_map/m2l/pallas_call | solution.py:209
  (20 shorter events, 0.1 us)
Async XLA Ops:
  7.2 88.7 %all-gather.3.cloned.1.call-start = ((), (), s32[]{:S(2)}) async-start(), calls=%async_computation | async-start | bytes 2228224 | tf_op jit(solution)/shard_map/all_gather | solution.py:254
  8.1 30.5 %copy-start.3 = (bf16[256,128]{1,0:T(8,128)(2,1)}, bf16[256,128]{1,0:T(8,128)(2,1)S(1)}, u32[]{:S(2)}) copy-start(bf16[256,128]{1,0:T(8,128)(2,1)S(1)} %get-tuple-element.25.own_hbm) | copy-start | bytes 196612
  8.1 4.1 %collective-permute-start.1 = (bf16[256,128]{1,0:T(8,128)(2,1)S(1)}, bf16[256,128]{1,0:T(8,128)(2,1)S(1)}, u32[]{:S(2)}, u32[]{:S(2)}) collective-permute-start(bf16[256,128]{1,0:T(8,128)(2,1)S(1)} %get-tuple-element.25.own_hbm), channel_id=1, source_target_pairs={{8,24},{9,25},{10,26},{11,27},{12,28},{13,29},{14,30},{15,31},{16,... | collective-permute-start | bytes 196616 | tf_op jit(solution)/shard_map/ppermute | solution.py:253
  14.9 23.6 %copy-start.1 = (f32[4,256,128]{2,1,0:T(8,128)}, f32[4,256,128]{2,1,0:T(8,128)S(1)}, u32[]{:S(2)}) copy-start(f32[4,256,128]{2,1,0:T(8,128)S(1)} %pad_maximum_fusion.own_ref) | copy-start | bytes 1572868
  14.9 28.3 %collective-permute-start = (f32[4,256,128]{2,1,0:T(8,128)S(1)}, f32[4,256,128]{2,1,0:T(8,128)S(1)}, u32[]{:S(2)}, u32[]{:S(2)}) collective-permute-start(f32[4,256,128]{2,1,0:T(8,128)S(1)} %pad_maximum_fusion.own_ref), channel_id=1, source_target_pairs={{1,0},{2,1},{3,2},{4,3},{5,4},{6,5},{7,6},{8,7},{9,8},{10,9},{11,1... | collective-permute-start | bytes 1572872 | tf_op jit(solution)/shard_map/ppermute | solution.py:237
  25.6 3.9 %copy-start = (bf16[316,121,121]{2,0,1:T(8,128)(2,1)S(1)}, bf16[316,121,121]{2,0,1:T(8,128)(2,1)}, u32[]{:S(2)}) copy-start(bf16[316,121,121]{2,0,1:T(8,128)(2,1)} %param.14) | copy-start | bytes 27759340
  29.6 9.0 %copy-start.4 = (s32[256,189]{0,1:T(8,128)S(1)}, s32[256,189]{0,1:T(8,128)}, u32[]{:S(2)}) copy-start(s32[256,189]{0,1:T(8,128)} %param.16) | copy-start | bytes 580612
  29.6 9.0 %copy-start.7 = (s32[256]{0:T(256)S(1)}, s32[256]{0:T(256)}, u32[]{:S(2)}) copy-start(s32[256]{0:T(256)} %param.18) | copy-start | bytes 3076
  29.6 9.8 %copy-start.5 = (s32[256,189]{0,1:T(8,128)S(1)}, s32[256,189]{0,1:T(8,128)}, u32[]{:S(2)}) copy-start(s32[256,189]{0,1:T(8,128)} %param.17) | copy-start | bytes 580612
  38.6 55.6 %copy-start.6 = (s32[256]{0:T(256)S(1)}, s32[256]{0:T(256)}, u32[]{:S(2)}) copy-start(s32[256]{0:T(256)} %param.21) | copy-start | bytes 3076
  43.3 0.8 copy-start.2
  83.5 10.7 %collective-permute-start.2 = (f32[256,128]{1,0:T(8,128)}, f32[256,128]{1,0:T(8,128)S(1)}, u32[]{:S(2)}, u32[]{:S(2)}) collective-permute-start(f32[256,128]{1,0:T(8,128)} %get-tuple-element.19), channel_id=1, source_target_pairs={{0,1},{1,2},{2,3},{3,4},{4,5},{5,6},{6,7},{7,8},{8,9},{9,10},{10,1... | collective-permute-start | bytes 393224 | tf_op jit(solution)/shard_map/ppermute | solution.py:237
Sparse Core Ops, SparseCore 0:
  13.0 54.2 all-gather.2
where the time goes:
time: 152 us; the launch traced here: 151 us
  Pallas kernels  97 us (64%)
  between operations  15.5 us (10%)
  starting transfers between devices  12.9 us (8%)
  waiting for transfers between devices  10.7 us (7%)
  other arithmetic  8.08 us (5%)
  local copies, waits for them, and re-layouts  7.24 us (5%)
    pallas_call x1, Pallas kernels, m2l(): pl.pallas_call(functools.partial(m2l_body, U, B, OG), out_shape=jax.Shape...  48.7 us
    pallas_call x1, Pallas kernels, near(): pl.pallas_call(functools.partial(near_body, U, PU), out_shape=(jax.ShapeD...  39.4 us
    ppermute x2, starting transfers between devices, ring(): lax.ppermute(x, AXES, [(i, i + by) for i in range(n) if 0 <= i + by < n])  10.6 us
    pallas_call x1, Pallas kernels, relayout(): pl.pallas_call(relayout_body, out_shape=jax.ShapeDtypeStruct((OP, 128, 12...  8.94 us
    ppermute x2, waiting for transfers between devices, ring(): lax.ppermute(x, AXES, [(i, i + by) for i in range(n) if 0 <= i + by < n])  8.79 us
    unnamed x20, local copies, waits for them, and re-layouts  6.38 us
  transfers between devices with their start and end apart: 4, of which 2 were waited for; matrix products, arithmetic and copies ran while one was open for 6% of the time, Pallas kernels for 32%

commit v1 on v0

--- a/solution.py
+++ b/solution.py
@@ -76,7 +76,10 @@
     lane=lax.broadcasted_iota(jnp.int32,(PB,128),1)
     if True:
         def pairs(g,_):
-            cs=[]
+            blk=lax.shift_right_logical(g*U,7)
+            l0=(g*U)&127
+            r=pl.ds(pl.multiple_of(blk*128,128),128)
+            c=cc[r,:]
             for u in range(U):
                 p=g*U+u
                 a=tgt_ref[p]; b=src_ref[p]; o=off_ref[p]
@@ -84,13 +87,7 @@
                 k=lax.rsqrt(jnp.dot(fa[a],feat_b(y),preferred_element_type=f32))
                 qb=xb[pl.ds(b*8+3,1),:]
                 dd[pl.ds(p,1),:]=jnp.sum(k*qa[a],axis=0,keepdims=True)
-                cs.append(jnp.sum(k*qb,axis=1,keepdims=True))
-            blk=lax.shift_right_logical(g*U,7)
-            l0=(g*U)&127
-            r=pl.ds(pl.multiple_of(blk*128,128),128)
-            c=cc[r,:]
-            for u in range(U):
-                c=jnp.where(lane==l0+u,cs[u],c)
+                c=jnp.where(lane==l0+u,jnp.sum(k*qb,axis=1,keepdims=True),c)
             cc[r,:]=c
             return 0
         lax.fori_loop(0,lax.div(n+U-1,U),pairs,0)
@@ -112,7 +109,7 @@
         return 0
     lax.fori_loop(0,lax.div(n+127,128),scat,0)
 
-def near(tgt,src,off,cnt,own4,nxt4,U=32,PU=16):
+def near(tgt,src,off,cnt,own4,nxt4,U=64,PU=32):
     sm=pl.BlockSpec(memory_space=pltpu.SMEM); vm=pl.BlockSpec(memory_space=pltpu.VMEM)
     return pl.pallas_call(functools.partial(near_body,U,PU),
         out_shape=(jax.ShapeDtypeStruct((BOX,PB),f32),jax.ShapeDtypeStruct((BOX,PB),f32)),
@@ -135,9 +132,6 @@
 
 def relayout_body(in_ref,out_ref,buf):
     OB=in_ref.shape[1]
-    @pl.when(pl.program_id(0)==0)
-    def _():
-        buf[...]=jnp.zeros_like(buf)
     for c in range(COEF):
         buf[c*OB:(c+1)*OB,:COEF]=in_ref[c].astype(f32)
     sub=lax.broadcasted_iota(jnp.int32,(8,128),0)
@@ -150,13 +144,17 @@
                 out_ref[o+i,c:c+16,:]=jnp.concatenate([lo[i],hi[i]],0).astype(bf16)
 
 def relayout(ops_t,OB=32):
-    return pl.pallas_call(relayout_body,
+    def outer(src,dst,buf):
+        buf[...]=jnp.zeros_like(buf)
+        pltpu.emit_pipeline(lambda i,o: relayout_body(i,o,buf),grid=(OP//OB,),
+            in_specs=[pl.BlockSpec((COEF,OB,COEF),lambda i:(0,i,0))],
+            out_specs=[pl.BlockSpec((OB,128,128),lambda i:(i,0,0))])(src,dst)
+    hb=pl.BlockSpec(memory_space=pltpu.HBM)
+    return pl.pallas_call(outer,
         out_shape=jax.ShapeDtypeStruct((OP,128,128),bf16),
-        grid=(OP//OB,),
-        in_specs=[pl.BlockSpec((COEF,OB,COEF),lambda i:(0,i,0))],
-        out_specs=pl.BlockSpec((OB,128,128),lambda i:(i,0,0)),
+        in_specs=[hb],out_specs=hb,
         scratch_shapes=[pltpu.VMEM((128*OB,128),f32)],
-        compiler_params=pltpu.CompilerParams(vmem_limit_bytes=40<<20),
+        compiler_params=pltpu.CompilerParams(vmem_limit_bytes=60<<20),
         name="relayout")(ops_t)
 
 def m2l_body(U,B,OG,num_ref,want_ref,blk_ref,src_hbm,dst_hbm,lst_hbm,own_hbm,ag_hbm,ops_hbm,out_ref,
@@ -263,6 +261,7 @@
     field,fwd=near(pair_target[0],pair_source[0],pair_offset[0],pair_count,own4,nxt4)
     back=ring(fwd,1,n)
     local_exp=m2l(s,d,lst,num,want_boxes.reshape(-1),blk,own,ag,ops)
+    local_exp,back,field=lax.optimization_barrier((local_exp,back,field))
     return local_exp,jnp.where(live,field+back,0.0)
 
 def solution(mesh):

time: 152 us -> 138 us (0.908)
  the two profiles are of different devices: /device:TPU:6 before, /device:TPU:5 now
where the time goes in v1:
time: 138 us
  Pallas kernels  95.7 us (69%)
  between operations  15.5 us (11%)
  starting transfers between devices  13.2 us (10%)
  other arithmetic  7.24 us (5%)
  local copies, waits for them, and re-layouts  3.32 us (2%)
  waiting for transfers between devices  3.04 us (2%)
    pallas_call x1, Pallas kernels, m2l(): pl.pallas_call(functools.partial(m2l_body, U, B, OG), out_shape=jax.Shape...  46.4 us
    pallas_call x1, Pallas kernels, near(): pl.pallas_call(functools.partial(near_body, U, PU), out_shape=(jax.ShapeD...  36.2 us
    pallas_call x1, Pallas kernels, relayout(): pl.pallas_call(outer, out_shape=jax.ShapeDtypeStruct((OP, 128, 128), bf16...  13.2 us
    ppermute x2, starting transfers between devices, ring(): lax.ppermute(x, AXES, [(i, i + by) for i in range(n) if 0 <= i + by < n])  10.6 us
    ppermute x1, waiting for transfers between devices, shards(): other = lax.ppermute(own, AXES, swap)  2.99 us
  transfers between devices with their start and end apart: 4, of which 1 were waited for; matrix products, arithmetic and copies ran while one was open for 5% of the time, Pallas kernels for 69%

profile of v1, /device:TPU:5, one launch (start us, length us, event | category | flops | bytes accessed | tf_op | source)
XLA Modules:
  0.0 138.1 jit_solution(6129515906461593993)
XLA Ops:
  7.2 0.0 all-gather.3.cloned.1.call-start
  7.2 0.9 pad_bitcast_fusion.2
  8.1 2.6 %collective-permute-start.1 = (bf16[256,128]{1,0:T(8,128)(2,1)S(1)}, bf16[256,128]{1,0:T(8,128)(2,1)S(1)}, u32[]{:S(2)}, u32[]{:S(2)}) collective-permute-start(bf16[256,128]{1,0:T(8,128)(2,1)S(1)} %get-tuple-element.31.own_hbm), channel_id=1, source_target_pairs={{8,24},{9,25},{10,26},{11,27},{12,28},{13,29},{14,30},{15,31},{16,... | collective-permute-start | bytes 196616 | tf_op jit(solution)/shard_map/ppermute | solution.py:251
  10.7 3.0 %collective-permute-done.1 = bf16[256,128]{1,0:T(8,128)(2,1)S(1)} collective-permute-done((bf16[256,128]{1,0:T(8,128)(2,1)S(1)}, bf16[256,128]{1,0:T(8,128)(2,1)S(1)}, u32[]{:S(2)}, u32[]{:S(2)}) %collective-permute-start.1) | collective-permute-done | bytes 65568 | tf_op jit(solution)/shard_map/ppermute | solution.py:251
  13.7 0.7 pad_maximum_fusion.1
  14.3 0.0 all-gather.3.cloned.1.call-update
  14.4 1.0 select_bitcast_fusion
  15.4 1.0 pad_maximum_fusion.own_ref
  16.4 8.7 %collective-permute-start = (f32[4,256,128]{2,1,0:T(8,128)S(1)}, f32[4,256,128]{2,1,0:T(8,128)S(1)}, u32[]{:S(2)}, u32[]{:S(2)}) collective-permute-start(f32[4,256,128]{2,1,0:T(8,128)S(1)} %pad_maximum_fusion.own_ref), channel_id=1, source_target_pairs={{1,0},{2,1},{3,2},{4,3},{5,4},{6,5},{7,6},{8,7},{9,8},{10,9},{11,1... | collective-permute-start | bytes 1572872 | tf_op jit(solution)/shard_map/ppermute | solution.py:235
  25.1 1.3 fusion.4
  27.1 0.0 copy-start.3
  27.1 13.2 %relayout.1 = bf16[320,128,128]{2,1,0:T(8,128)(2,1)} custom-call(bf16[121,316,121]{2,1,0:T(8,128)(2,1)} %bitcast.27), custom_call_target="tpu_custom_call" | custom-call | tf_op jit(solution)/shard_map/relayout/pallas_call | solution.py:153
  40.4 0.8 copy.15
  41.2 0.8 copy.16
  42.7 0.1 select_reduce_fusion.1
  42.8 0.6 fusion.3.blk_ref
  43.4 1.1 select_reduce_fusion
  44.5 0.6 add_select_fusion.1.lst_hbm
  45.1 0.8 copy-done.1
  45.9 36.2 %near.1 = (f32[256,128]{1,0:T(8,128)}, f32[256,128]{1,0:T(8,128)}) custom-call(s32[1024]{0:T(1024)} %bitcast.33, s32[1024]{0:T(1024)} %bitcast.35, s32[1024]{0:T(1024)} %bitcast.38, s32[1]{0:T(128)S(6)} %copy.17.cnt_ref, f32[4,256,128]{2,1,0:T(8,128)} %copy-done, f32[4,256,128]{2,1,0:T(8,128)} %copy-done.1, s32[8,128]{1,0:T(8,128)} %bitcast.34, ...), custom_call_target="tpu_custom_call" | custom-call | tf_op jit(solution)/shard_map/near/pallas_call | solution.py:114
  82.1 1.9 %collective-permute-start.2 = (f32[256,128]{1,0:T(8,128)}, f32[256,128]{1,0:T(8,128)S(1)}, u32[]{:S(2)}, u32[]{:S(2)}) collective-permute-start(f32[256,128]{1,0:T(8,128)} %get-tuple-element.21), channel_id=1, source_target_pairs={{0,1},{1,2},{2,3},{3,4},{4,5},{5,6},{6,7},{7,8},{8,9},{9,10},{10,1... | collective-permute-start | bytes 393224 | tf_op jit(solution)/shard_map/ppermute | solution.py:235
  84.0 0.0 all-gather.3.cloned.1.call-done
  84.0 46.4 %m2l.1 = f32[256,121]{1,0:T(8,128)} custom-call(s32[1]{0:T(128)} %bitcast.6.num_ref, s32[2048]{0:T(1024)} %bitcast.37, s32[16]{0:T(128)} %fusion.3.blk_ref, s32[53248]{0:T(1024)} %bitcast.29, s32[53248]{0:T(1024)} %bitcast.30, s32[3200]{0:T(1024)} %add_select_fusion.1.lst_hbm, bf16[256,128]{1,0:T(8,128)(2,1)} %copy-done.2, bf16[8192,128]{1,0:T(8,128)(2,1)} %bitcast.28, ...), custom_call_target="tpu_custom_call" | custom-call | tf_op jit(solution)/shard_map/m2l/pallas_call | solution.py:207
  130.5 0.8 add_select_fusion
  (20 shorter events, 0.1 us)
Async XLA Ops:
  7.2 76.8 %all-gather.3.cloned.1.call-start = ((), (), s32[]{:S(2)}) async-start(), calls=%async_computation | async-start | bytes 2228224 | tf_op jit(solution)/shard_map/all_gather | solution.py:252
  8.1 32.2 %copy-start.2 = (bf16[256,128]{1,0:T(8,128)(2,1)}, bf16[256,128]{1,0:T(8,128)(2,1)S(1)}, u32[]{:S(2)}) copy-start(bf16[256,128]{1,0:T(8,128)(2,1)S(1)} %get-tuple-element.31.own_hbm) | copy-start | bytes 196612
  8.1 5.6 %collective-permute-start.1 = (bf16[256,128]{1,0:T(8,128)(2,1)S(1)}, bf16[256,128]{1,0:T(8,128)(2,1)S(1)}, u32[]{:S(2)}, u32[]{:S(2)}) collective-permute-start(bf16[256,128]{1,0:T(8,128)(2,1)S(1)} %get-tuple-element.31.own_hbm), channel_id=1, source_target_pairs={{8,24},{9,25},{10,26},{11,27},{12,28},{13,29},{14,30},{15,31},{16,... | collective-permute-start | bytes 196616 | tf_op jit(solution)/shard_map/ppermute | solution.py:251
  16.4 23.9 %copy-start = (f32[4,256,128]{2,1,0:T(8,128)}, f32[4,256,128]{2,1,0:T(8,128)S(1)}, u32[]{:S(2)}) copy-start(f32[4,256,128]{2,1,0:T(8,128)S(1)} %pad_maximum_fusion.own_ref) | copy-start | bytes 1572868
  16.4 28.6 %collective-permute-start = (f32[4,256,128]{2,1,0:T(8,128)S(1)}, f32[4,256,128]{2,1,0:T(8,128)S(1)}, u32[]{:S(2)}, u32[]{:S(2)}) collective-permute-start(f32[4,256,128]{2,1,0:T(8,128)S(1)} %pad_maximum_fusion.own_ref), channel_id=1, source_target_pairs={{1,0},{2,1},{3,2},{4,3},{5,4},{6,5},{7,6},{8,7},{9,8},{10,9},{11,1... | collective-permute-start | bytes 1572872 | tf_op jit(solution)/shard_map/ppermute | solution.py:235
  27.1 13.2 %copy-start.3 = (s32[256,189]{0,1:T(8,128)S(1)}, s32[256,189]{0,1:T(8,128)}, u32[]{:S(2)}) copy-start(s32[256,189]{0,1:T(8,128)} %param.16) | copy-start | bytes 580612
  27.1 13.2 %copy-start.7 = (s32[256]{0:T(256)S(1)}, s32[256]{0:T(256)}, u32[]{:S(2)}) copy-start(s32[256]{0:T(256)} %param.18) | copy-start | bytes 3076
  27.1 14.0 %copy-start.4 = (s32[256,189]{0,1:T(8,128)S(1)}, s32[256,189]{0,1:T(8,128)}, u32[]{:S(2)}) copy-start(s32[256,189]{0,1:T(8,128)} %param.17) | copy-start | bytes 580612
  45.1 0.8 copy-start.1
  82.1 48.4 %collective-permute-start.2 = (f32[256,128]{1,0:T(8,128)}, f32[256,128]{1,0:T(8,128)S(1)}, u32[]{:S(2)}, u32[]{:S(2)}) collective-permute-start(f32[256,128]{1,0:T(8,128)} %get-tuple-element.21), channel_id=1, source_target_pairs={{0,1},{1,2},{2,3},{3,4},{4,5},{5,6},{6,7},{7,8},{8,9},{9,10},{10,1... | collective-permute-start | bytes 393224 | tf_op jit(solution)/shard_map/ppermute | solution.py:235
  84.0 46.4 %copy-start.5 = (f32[256,128]{1,0:T(8,128)S(1)}, f32[256,128]{1,0:T(8,128)}, u32[]{:S(2)}) copy-start(f32[256,128]{1,0:T(8,128)} %get-tuple-element.24) | copy-start | bytes 393220
  84.0 46.4 %copy-start.6 = (s32[256]{0:T(256)S(1)}, s32[256]{0:T(256)}, u32[]{:S(2)}) copy-start(s32[256]{0:T(256)} %param.21) | copy-start | bytes 3076
Sparse Core Ops, SparseCore 0:
  14.5 51.7 all-gather.2

commit v2 on v1

--- a/solution.py
+++ b/solution.py
@@ -21,7 +21,11 @@
     b=r.astype(bf16).astype(f32); c=r-b
     return a,b,c
 
-def near_body(U,PU,tgt_ref,src_ref,off_ref,cnt_ref,own_ref,nxt_ref,tcol_ref,srow_ref,out_ref,fwd_ref,xb,fa,qa,cc,dd,vv):
+NCLS=4
+LSEG=2048
+NPOS=1408
+
+def near_body(U,PU,prs_ref,own_ref,nxt_ref,out_ref,fwd_ref,xb,fa,qa,cc,dd,vv,ids,lst,num):
     sub=lax.broadcasted_iota(jnp.int32,(8,128),0)
     m3=(sub<3).astype(f32)
     one=jnp.ones((8,128),f32); zero=jnp.zeros((8,128),f32)
@@ -45,6 +49,14 @@
     diag=lax.broadcasted_iota(jnp.int32,(PB,PB),0)==lax.broadcasted_iota(jnp.int32,(PB,PB),1)
     def sq(b):
         return xb[pl.ds(pl.multiple_of(b*8,8),8),:]
+    for c in range(NCLS+1): num[c]=0
+    def sort_pair(p):
+        w=prs_ref[p]
+        c=lax.shift_right_logical(w,22)
+        k=num[c]
+        lst[c*LSEG+k]=w
+        num[c]=k+1
+    PP=1024//(BOX//PU)//PU
     def prep(g,_):
         for u in range(PU):
             b=g*PU+u
@@ -65,40 +77,52 @@
             k=lax.rsqrt(jnp.dot(ft,feat_b(x),preferred_element_type=f32))
             k=jnp.where(diag,0.0,k)
             out_ref[pl.ds(b,1),:]=jnp.sum(k*q,axis=0,keepdims=True)
+            for v in range(PP): sort_pair(g*(PU*PP)+u*PP+v)
         return 0
     lax.fori_loop(0,BOX//PU,prep,0)
-    n=cnt_ref[0]
     def zinit(i,_):
         dd[pl.ds(pl.multiple_of(i*8,8),8),:]=zero
         cc[pl.ds(pl.multiple_of(i*8,8),8),:]=zero
         return 0
-    lax.fori_loop(0,128,zinit,0)
-    lane=lax.broadcasted_iota(jnp.int32,(PB,128),1)
-    if True:
+    lax.fori_loop(0,NPOS//8,zinit,0)
+    ids[...]=jnp.full_like(ids,-1)
+    lane1=lax.broadcasted_iota(jnp.int32,(1,128),1)
+    base=jnp.int32(0)
+    for cl in range(NCLS):
+        R=PB//NCLS*(cl+1)
+        lane=lax.broadcasted_iota(jnp.int32,(R,128),1)
+        m=num[cl]
         def pairs(g,_):
-            blk=lax.shift_right_logical(g*U,7)
-            l0=(g*U)&127
-            r=pl.ds(pl.multiple_of(blk*128,128),128)
+            p0=base+g*U
+            blk=lax.shift_right_logical(p0,7)
+            l0=p0&127
+            r=pl.ds(pl.multiple_of(blk*128,128),R)
             c=cc[r,:]
+            ti=ids[pl.ds(blk,1),:]
+            si=ids[pl.ds(16+blk,1),:]
             for u in range(U):
-                p=g*U+u
-                a=tgt_ref[p]; b=src_ref[p]; o=off_ref[p]
+                ok=g*U+u<m
+                pk=jnp.where(ok,lst[cl*LSEG+g*U+u],0)
+                a=pk&255; b=lax.shift_right_logical(pk,8)&511; o=lax.shift_right_logical(pk,17)&31
                 y=sq(b)+vv[o]
-                k=lax.rsqrt(jnp.dot(fa[a],feat_b(y),preferred_element_type=f32))
+                k=lax.rsqrt(jnp.dot(fa[a,0:R,:],feat_b(y),preferred_element_type=f32))
                 qb=xb[pl.ds(b*8+3,1),:]
-                dd[pl.ds(p,1),:]=jnp.sum(k*qa[a],axis=0,keepdims=True)
+                dd[pl.ds(p0+u,1),:]=jnp.sum(k*qa[a,0:R,:],axis=0,keepdims=True)
                 c=jnp.where(lane==l0+u,jnp.sum(k*qb,axis=1,keepdims=True),c)
+                ti=jnp.where(lane1==l0+u,jnp.where(ok,a,-1),ti)
+                si=jnp.where(lane1==l0+u,jnp.where(ok,b,-1),si)
             cc[r,:]=c
+            ids[pl.ds(blk,1),:]=ti
+            ids[pl.ds(16+blk,1),:]=si
             return 0
-        lax.fori_loop(0,lax.div(n+U-1,U),pairs,0)
+        it=lax.div(m+U-1,U)
+        lax.fori_loop(0,it,pairs,0)
+        base=base+it*U
     fwd_ref[...]=jnp.zeros_like(fwd_ref)
     def scat(k,_):
         r=pl.ds(pl.multiple_of(k*128,128),128)
-        prow=k*128+lax.broadcasted_iota(jnp.int32,(1,128),1)
-        tid=jnp.where(prow<n,tcol_ref[pl.ds(k,1),:],-1)
-        sid=jnp.where(prow<n,srow_ref[pl.ds(k,1),:],-1)
-        oh_t=(lax.broadcasted_iota(jnp.int32,(BOX,128),0)==tid).astype(f32).astype(bf16)
-        oh_s=(lax.broadcasted_iota(jnp.int32,(2*BOX,128),0)==sid).astype(f32).astype(bf16)
+        oh_t=(lax.broadcasted_iota(jnp.int32,(BOX,128),0)==ids[pl.ds(k,1),:]).astype(f32).astype(bf16)
+        oh_s=(lax.broadcasted_iota(jnp.int32,(2*BOX,128),0)==ids[pl.ds(16+k,1),:]).astype(f32).astype(bf16)
         c1,c2,c3=split3(cc[r,:])
         d1,d2,d3=split3(dd[r,:])
         nt=(((1,),(1,)),((),()))
@@ -107,18 +131,29 @@
         out_ref[...]+=ct+ds[:BOX]
         fwd_ref[...]+=ds[BOX:]
         return 0
-    lax.fori_loop(0,lax.div(n+127,128),scat,0)
-
-def near(tgt,src,off,cnt,own4,nxt4,U=64,PU=32):
+    lax.fori_loop(0,lax.div(base+127,128),scat,0)
+
+def pair_words(tgt,src,off,cnt,pc):
+    box=jnp.arange(BOX,dtype=jnp.int32)[None,:]
+    na=jnp.sum(jnp.where(tgt[:,None]==box,pc[None,:],0),1)
+    nb=jnp.sum(jnp.where(src[:,None]==box,pc[None,:],0),1)
+    sw=(src<BOX)&(nb<na)
+    a,b,o=jnp.where(sw,src,tgt),jnp.where(sw,tgt,src),jnp.where(sw,26-off,off)
+    c=(jnp.where(sw,nb,na)-1)>>5
+    c=jnp.where(jnp.arange(tgt.shape[0],dtype=jnp.int32)<cnt[0],c,NCLS)
+    return a+b*256+o*131072+c*4194304
+
+def near(prs,own4,nxt4,U=128,PU=32):
     sm=pl.BlockSpec(memory_space=pltpu.SMEM); vm=pl.BlockSpec(memory_space=pltpu.VMEM)
     return pl.pallas_call(functools.partial(near_body,U,PU),
         out_shape=(jax.ShapeDtypeStruct((BOX,PB),f32),jax.ShapeDtypeStruct((BOX,PB),f32)),
-        in_specs=[sm]*4+[vm]*4,
+        in_specs=[sm]+[vm]*2,
         out_specs=(vm,vm),
         scratch_shapes=[pltpu.VMEM((2*BOX*8,128),f32),pltpu.VMEM((BOX,PB,128),bf16),pltpu.VMEM((BOX,PB,128),f32),
-            pltpu.VMEM((1024,128),f32),pltpu.VMEM((1024,128),f32),pltpu.VMEM((27,8,128),f32)],
+            pltpu.VMEM((NPOS,128),f32),pltpu.VMEM((NPOS,128),f32),pltpu.VMEM((27,8,128),f32),pltpu.VMEM((32,128),jnp.int32),
+            pltpu.SMEM(((NCLS+1)*LSEG,),jnp.int32),pltpu.SMEM((8,),jnp.int32)],
         compiler_params=pltpu.CompilerParams(vmem_limit_bytes=56<<20),
-        name="near")(tgt,src,off,cnt,own4,nxt4,tgt.reshape(8,128),src.reshape(8,128))
+        name="near")(prs,own4,nxt4)
 
 def swap8(rows,masks):
     rows=list(rows)
@@ -147,7 +182,7 @@
     def outer(src,dst,buf):
         buf[...]=jnp.zeros_like(buf)
         pltpu.emit_pipeline(lambda i,o: relayout_body(i,o,buf),grid=(OP//OB,),
-            in_specs=[pl.BlockSpec((COEF,OB,COEF),lambda i:(0,i,0))],
+            in_specs=[pl.BlockSpec((COEF,OB,COEF),lambda i:(0,i,0),pipeline_mode=pl.Buffered(3))],
             out_specs=[pl.BlockSpec((OB,128,128),lambda i:(i,0,0))])(src,dst)
     hb=pl.BlockSpec(memory_space=pltpu.HBM)
     return pl.pallas_call(outer,
@@ -185,7 +220,8 @@
         for v in range(B):
             b=lst_ref.at[pl.ds(v,3072)][i*B]
             for u in range(U):
-                w=pl.ds(u*BOX,(KP-U)*BOX+BOX)
+                off=(u//8)*2048+(u%8)*128
+                w=pl.ds(off,KP*BOX-off)
                 dense[pl.ds(dst_ref.at[w][b],1),:]=tab[pl.ds(src_ref.at[w][b],1),:]
         return 0
     lax.fori_loop(0,num_ref[0],chunk,0)
@@ -218,16 +254,19 @@
     t=lax.broadcasted_iota(jnp.int32,(KMAX,BOX),1)
     s=jnp.where(k<cnt[None,:],srcT,ZROW)
     d=offT*BOX+t
-    s=jnp.pad(s,((0,KP-KMAX),(0,0)),constant_values=ZROW).reshape(-1)
-    d=jnp.pad(d,((0,KP-KMAX),(0,0)),constant_values=DROW).reshape(-1)
+    def tiled(x,fill):
+        x=jnp.pad(x,((0,KP-KMAX),(0,0)),constant_values=fill)
+        return x.reshape(KP//8,8,BOX//128,128).transpose(0,2,1,3).reshape(-1)
+    s=tiled(s,ZROW)
+    d=tiled(d,DROW)
     n=lax.div(cnt+U-1,U)
     a=jnp.arange(BOX,dtype=jnp.int32)
     incl=jnp.sum(jnp.where(a[None,:]<=a[:,None],n[None,:],0),1)
     i=jnp.arange(LST,dtype=jnp.int32)
     m=incl[None,:]<=i[:,None]
     bx=jnp.sum(m.astype(jnp.int32),1)
-    ex=jnp.sum(jnp.where(m,n[None,:],0),1)
-    lst=jnp.where(bx<BOX,bx+(i-ex)*(U*BOX),192*BOX)
+    c=i-jnp.sum(jnp.where(m,n[None,:],0),1)
+    lst=jnp.where(bx<BOX,c*4096+(bx>>7)*1024+(bx&127),192*BOX)
     num=lax.div(jnp.sum(n)+B-1,B)
     return s,d,lst,num[None]
 
@@ -240,7 +279,6 @@
     x,y=lax.axis_index("gx"),lax.axis_index("gy")
     live=lax.broadcasted_iota(jnp.int32,(BOX,PB),1)<part_count[:,None]
     own4=jnp.concatenate([positions.transpose(1,0,2),jnp.where(live,charges,0.0)[None]],0)
-    nxt4=ring(own4,-1,n)
     own=jnp.pad(multipoles,((0,0),(0,128-COEF)))
     half=gy//2
     swap=[]
@@ -249,6 +287,8 @@
             to=g+1 if j>=half else g-1
             if 0<=to<gx: swap.append((g*gy+j,to*gy+j))
     other=lax.ppermute(own,AXES,swap)
+    nxt4=ring(own4,-1,n)
+    other,_=lax.optimization_barrier((other,own4))
     ag=lax.all_gather(jnp.stack([own,other]),"gy").reshape(-1,128)
     me=x*gy+y
     reach=jnp.arange(NEAR,dtype=jnp.int32)
@@ -257,8 +297,9 @@
     blk=py*2+(px!=x).astype(jnp.int32)
     s,d,lst,num=slots(m2l_source.T,m2l_offset.T,m2l_count)
     ops=relayout(m2l_ops.transpose(1,0,2)).reshape(-1,128)
-    nxt4,ops,s,d,lst,num,blk=lax.optimization_barrier((nxt4,ops,s,d,lst,num,blk))
-    field,fwd=near(pair_target[0],pair_source[0],pair_offset[0],pair_count,own4,nxt4)
+    prs=pair_words(pair_target[0],pair_source[0],pair_offset[0],pair_count,part_count)
+    nxt4,ops,s,d,lst,num,blk,prs=lax.optimization_barrier((nxt4,ops,s,d,lst,num,blk,prs))
+    field,fwd=near(prs,own4,nxt4)
     back=ring(fwd,1,n)
     local_exp=m2l(s,d,lst,num,want_boxes.reshape(-1),blk,own,ag,ops)
     local_exp,back,field=lax.optimization_barrier((local_exp,back,field))

time: 138 us -> 130 us (0.942)
  the two profiles are of different devices: /device:TPU:5 before, /device:TPU:90 now
where the time goes in v2:
time: 130 us; the launch traced here: 131 us
  Pallas kernels  86.7 us (67%)
  between operations  15.5 us (12%)
  starting transfers between devices  15 us (12%)
  other arithmetic  8.82 us (7%)
  local copies, waits for them, and re-layouts  3.14 us (2%)
  waiting for transfers between devices  1.63 us (1%)
    pallas_call x1, Pallas kernels, m2l(): pl.pallas_call(functools.partial(m2l_body, U, B, OG), out_shape=jax.Shape...  46.3 us
    pallas_call x1, Pallas kernels, near(): pl.pallas_call(functools.partial(near_body, U, PU), out_shape=(jax.ShapeD...  30.4 us
    ppermute x2, starting transfers between devices, ring(): lax.ppermute(x, AXES, [(i, i + by) for i in range(n) if 0 <= i + by < n])  13.1 us
    pallas_call x1, Pallas kernels, relayout(): pl.pallas_call(outer, out_shape=jax.ShapeDtypeStruct((OP, 128, 128), bf16...  10 us
  transfers between devices with their start and end apart: 4, of which 1 were waited for; matrix products, arithmetic and copies ran while one was open for 7% of the time, Pallas kernels for 66%

profile of v2, /device:TPU:90, one launch (start us, length us, event | category | flops | bytes accessed | tf_op | source)
XLA Modules:
  0.0 130.9 jit_solution(7856634399078627770)
XLA Ops:
  7.2 0.0 all-gather.3.cloned.1.call-start
  7.2 0.9 pad_bitcast_fusion
  8.1 1.9 %collective-permute-start.1 = (bf16[256,128]{1,0:T(8,128)(2,1)S(1)}, bf16[256,128]{1,0:T(8,128)(2,1)S(1)}, u32[]{:S(2)}, u32[]{:S(2)}) collective-permute-start(bf16[256,128]{1,0:T(8,128)(2,1)S(1)} %get-tuple-element.37.own_hbm), channel_id=1, source_target_pairs={{8,24},{9,25},{10,26},{11,27},{12,28},{13,29},{14,30},{15,31},{16,... | collective-permute-start | bytes 196616 | tf_op jit(solution)/shard_map/ppermute | solution.py:289
  10.0 1.0 select_bitcast_fusion
  11.0 1.0 pad_maximum_fusion.own_ref
  12.1 1.6 %collective-permute-done.1 = bf16[256,128]{1,0:T(8,128)(2,1)S(1)} collective-permute-done((bf16[256,128]{1,0:T(8,128)(2,1)S(1)}, bf16[256,128]{1,0:T(8,128)(2,1)S(1)}, u32[]{:S(2)}, u32[]{:S(2)}) %collective-permute-start.1) | collective-permute-done | bytes 65568 | tf_op jit(solution)/shard_map/ppermute | solution.py:289
  13.7 0.7 pad_maximum_fusion.1
  14.4 2.7 %collective-permute-start = (f32[4,256,128]{2,1,0:T(8,128)S(1)}, f32[4,256,128]{2,1,0:T(8,128)S(1)}, u32[]{:S(2)}, u32[]{:S(2)}) collective-permute-start(f32[4,256,128]{2,1,0:T(8,128)S(1)} %pad_maximum_fusion.own_ref), channel_id=1, source_target_pairs={{1,0},{2,1},{3,2},{4,3},{5,4},{6,5},{7,6},{8,7},{9,8},{10,9},{11,1... | collective-permute-start | bytes 1572872 | tf_op jit(solution)/shard_map/ppermute | solution.py:274
  17.0 1.3 %fusion.9 = (s32[]{:T(128)}, s32[256]{0:T(256)S(1)}) fusion(s32[256]{0:T(256)} %param.18), kind=kLoop, calls=%fused_computation.39 | loop fusion | flops 2047 | bytes 2052 | tf_op jit(solution)/shard_map/reduce_sum | solution.py:270
  19.7 10.0 %relayout.1 = bf16[320,128,128]{2,1,0:T(8,128)(2,1)} custom-call(bf16[121,316,121]{2,1,0:T(8,128)(2,1)} %bitcast.31), custom_call_target="tpu_custom_call" | custom-call | tf_op jit(solution)/shard_map/relayout/pallas_call | solution.py:188
  29.8 0.7 pad.12
  30.5 0.7 pad.11
  31.2 0.1 select_reduce_fusion.3
  31.3 1.0 select_reduce_fusion.1
  32.3 1.1 select_reduce_fusion
  33.4 0.6 fusion.8.blk_ref
  34.0 0.6 fusion.2.prs_ref
  34.6 0.6 add_select_fusion.1.lst_hbm
  35.2 0.8 copy-done.1
  36.1 30.4 %near.1 = (f32[256,128]{1,0:T(8,128)}, f32[256,128]{1,0:T(8,128)}) custom-call(s32[1024]{0:T(1024)} %fusion.2.prs_ref, f32[4,256,128]{2,1,0:T(8,128)} %copy-done, f32[4,256,128]{2,1,0:T(8,128)} %copy-done.1), custom_call_target="tpu_custom_call" | custom-call | tf_op jit(solution)/shard_map/near/pallas_call | solution.py:148
  66.5 10.4 %collective-permute-start.2 = (f32[256,128]{1,0:T(8,128)}, f32[256,128]{1,0:T(8,128)S(1)}, u32[]{:S(2)}, u32[]{:S(2)}) collective-permute-start(f32[256,128]{1,0:T(8,128)} %get-tuple-element.25), channel_id=1, source_target_pairs={{0,1},{1,2},{2,3},{3,4},{4,5},{5,6},{6,7},{7,8},{8,9},{9,10},{10,1... | collective-permute-start | bytes 393224 | tf_op jit(solution)/shard_map/ppermute | solution.py:274
  76.9 0.0 all-gather.3.cloned.1.call-done
  77.0 46.3 %m2l.1 = f32[256,121]{1,0:T(8,128)} custom-call(s32[1]{0:T(128)} %bitcast.12.num_ref, s32[2048]{0:T(1024)} %bitcast.41, s32[16]{0:T(128)} %fusion.8.blk_ref, s32[53248]{0:T(1024)} %bitcast.34, s32[53248]{0:T(1024)} %bitcast.33, s32[3200]{0:T(1024)} %add_select_fusion.1.lst_hbm, bf16[256,128]{1,0:T(8,128)(2,1)} %copy-done.2, bf16[8192,128]{1,0:T(8,128)(2,1)} %bitcast.32, ...), custom_call_target="tpu_custom_call" | custom-call | tf_op jit(solution)/shard_map/m2l/pallas_call | solution.py:243
  123.3 0.8 add_select_fusion
  (26 shorter events, 0.1 us)
Async XLA Ops:
  7.2 69.8 %all-gather.3.cloned.1.call-start = ((), (), s32[]{:S(2)}) async-start(), calls=%async_computation | async-start | bytes 2228224 | tf_op jit(solution)/shard_map/all_gather | solution.py:292
  8.1 21.7 %copy-start.2 = (bf16[256,128]{1,0:T(8,128)(2,1)}, bf16[256,128]{1,0:T(8,128)(2,1)S(1)}, u32[]{:S(2)}) copy-start(bf16[256,128]{1,0:T(8,128)(2,1)S(1)} %get-tuple-element.37.own_hbm) | copy-start | bytes 196612
  8.1 5.6 %collective-permute-start.1 = (bf16[256,128]{1,0:T(8,128)(2,1)S(1)}, bf16[256,128]{1,0:T(8,128)(2,1)S(1)}, u32[]{:S(2)}, u32[]{:S(2)}) collective-permute-start(bf16[256,128]{1,0:T(8,128)(2,1)S(1)} %get-tuple-element.37.own_hbm), channel_id=1, source_target_pairs={{8,24},{9,25},{10,26},{11,27},{12,28},{13,29},{14,30},{15,31},{16,... | collective-permute-start | bytes 196616 | tf_op jit(solution)/shard_map/ppermute | solution.py:289
  12.1 17.7 %copy-start = (f32[4,256,128]{2,1,0:T(8,128)}, f32[4,256,128]{2,1,0:T(8,128)S(1)}, u32[]{:S(2)}) copy-start(f32[4,256,128]{2,1,0:T(8,128)S(1)} %pad_maximum_fusion.own_ref) | copy-start | bytes 1572868
  14.4 20.9 %collective-permute-start = (f32[4,256,128]{2,1,0:T(8,128)S(1)}, f32[4,256,128]{2,1,0:T(8,128)S(1)}, u32[]{:S(2)}, u32[]{:S(2)}) collective-permute-start(f32[4,256,128]{2,1,0:T(8,128)S(1)} %pad_maximum_fusion.own_ref), channel_id=1, source_target_pairs={{1,0},{2,1},{3,2},{4,3},{5,4},{6,5},{7,6},{8,7},{9,8},{10,9},{11,1... | collective-permute-start | bytes 1572872 | tf_op jit(solution)/shard_map/ppermute | solution.py:274
  19.7 10.1 %copy-start.3 = (s32[256,189]{0,1:T(8,128)S(1)}, s32[256,189]{0,1:T(8,128)}, u32[]{:S(2)}) copy-start(s32[256,189]{0,1:T(8,128)} %param.17) | copy-start | bytes 580612
  19.7 10.8 %copy-start.4 = (s32[256,189]{0,1:T(8,128)S(1)}, s32[256,189]{0,1:T(8,128)}, u32[]{:S(2)}) copy-start(s32[256,189]{0,1:T(8,128)} %param.16) | copy-start | bytes 580612
  19.7 10.8 %copy-start.9 = (s32[256]{0:T(256)S(1)}, s32[256]{0:T(256)}, u32[]{:S(2)}) copy-start(s32[256]{0:T(256)} %param.18) | copy-start | bytes 3076
  19.7 11.6 %copy-start.6 = (s32[1,1024]{1,0:T(1,128)S(1)}, s32[1,1024]{1,0:T(1,128)}, u32[]{:S(2)}) copy-start(s32[1,1024]{1,0:T(1,128)} %param.22) | copy-start | bytes 12292
  19.7 11.6 %copy-start.7 = (s32[1,1024]{1,0:T(1,128)S(1)}, s32[1,1024]{1,0:T(1,128)}, u32[]{:S(2)}) copy-start(s32[1,1024]{1,0:T(1,128)} %param.23) | copy-start | bytes 12292
  19.7 11.6 %copy-start.8 = (s32[256]{0:T(256)S(1)}, s32[256]{0:T(256)}, u32[]{:S(2)}) copy-start(s32[256]{0:T(256)} %param.21) | copy-start | bytes 3076
  19.7 14.3 %copy-start.10 = (s32[1,1024]{1,0:T(1,128)S(1)}, s32[1,1024]{1,0:T(1,128)}, u32[]{:S(2)}) copy-start(s32[1,1024]{1,0:T(1,128)} %param.24) | copy-start | bytes 12292
  35.2 0.8 copy-start.1
  66.5 56.7 %collective-permute-start.2 = (f32[256,128]{1,0:T(8,128)}, f32[256,128]{1,0:T(8,128)S(1)}, u32[]{:S(2)}, u32[]{:S(2)}) collective-permute-start(f32[256,128]{1,0:T(8,128)} %get-tuple-element.25), channel_id=1, source_target_pairs={{0,1},{1,2},{2,3},{3,4},{4,5},{5,6},{6,7},{7,8},{8,9},{9,10},{10,1... | collective-permute-start | bytes 393224 | tf_op jit(solution)/shard_map/ppermute | solution.py:274
  77.0 46.3 %copy-start.5 = (f32[256,128]{1,0:T(8,128)S(1)}, f32[256,128]{1,0:T(8,128)}, u32[]{:S(2)}) copy-start(f32[256,128]{1,0:T(8,128)} %get-tuple-element.28) | copy-start | bytes 393220
Sparse Core Ops, SparseCore 0:
  14.5 47.1 all-gather.2
